TPU v7x, 128 devices: a whole 4x4x4 slice. The times are simulated.
128 devices in a mesh: real: 4 (over y), cell: 32 (over z, x, core).
Axes of the slice: x: 4, y: 4, z: 4, core: 2. Of those that a mesh axis runs over, the one named last changes fastest.
Arguments:
- snapshots: bfloat16 [8, 2, 256, 65536], P('real', None, None, 'cell'), may hold values from -6 to 6
- quad_weights: int32 [65536], P('cell'), may hold values from 1 to 11
- triad_pairs: int32 [512, 2], replicated, may hold values from 1 to 62, as said below
- owner_counts: int32 [32], replicated, may hold values from 1 to 32, 512 in all
Outputs:
- bispectra: float32 [1024, 8, 8, 2], P('cell', 'real')
Inputs may be any that keep to these rules, and one draw needn't show every extreme that they name: `owner_counts`: the counts sum to 512, each is at least 1, and the largest is exactly 32. `triad_pairs`: for each triad k >= 1, l >= 1 and k + l <= 63.
All inputs are finite; a program needn't handle non-finite values.
Results may differ from a plain program's by a relative error of at most 0.0075.
Values may be sent and summed in bfloat16 or wider, within the bound.
No kernel may reach another device: no remote copies, remote signals or barrier semaphores. Data moves between devices by JAX's collectives and lax.ppermute only.
A program may use at most 64 MiB of HBM per device.

v0:
```python
import jax
import jax.numpy as jnp
from jax import lax
from jax.sharding import PartitionSpec as P

FREQS = 64
TRI_DEV = 16
OWN_MOST = 32


def dft_table(steps_total, freq_total):
    times = jnp.arange(steps_total, dtype=jnp.int32)
    bins = jnp.arange(freq_total, dtype=jnp.int32)
    window = 0.5 - 0.5 * jnp.cos(2.0 * jnp.pi * times.astype(jnp.float32) / steps_total)
    window_norm = jnp.sqrt(jnp.sum(window * window))
    phases = (
        2.0
        * jnp.pi
        * (bins[:, None] * times[None, :] % steps_total).astype(jnp.float32)
        / steps_total
    )
    cos_rows = window[None, :] * jnp.cos(phases) / window_norm
    sin_rows = -window[None, :] * jnp.sin(phases) / window_norm
    return jnp.concatenate([cos_rows, sin_rows], axis=0).astype(jnp.bfloat16)


def select_bins(coefs, freq_ids):
    bin_ids = jnp.arange(coefs.shape[3], dtype=jnp.int32)
    onehot = (freq_ids[:, None] == bin_ids[None, :]).astype(jnp.bfloat16)
    return jnp.einsum("bf,ivcfx->ivcbx", onehot, coefs, preferred_element_type=jnp.float32)


def triad_block(row_coefs, col_coefs, weights, pair_block):
    first_freq = pair_block[:, 0]
    second_freq = pair_block[:, 1]
    sum_freq = first_freq + second_freq
    first_coef = select_bins(row_coefs, first_freq)
    second_coef = select_bins(row_coefs, second_freq)
    partner = select_bins(col_coefs, sum_freq).astype(jnp.bfloat16)
    prod_real = (
        first_coef[:, :, 0] * second_coef[:, :, 0] - first_coef[:, :, 1] * second_coef[:, :, 1]
    ) * weights
    prod_imag = (
        -(first_coef[:, :, 0] * second_coef[:, :, 1] + first_coef[:, :, 1] * second_coef[:, :, 0])
        * weights
    )
    product = jnp.stack([prod_real, prod_imag], axis=2).astype(jnp.bfloat16)
    against_real = jnp.stack([partner[:, :, 0], -partner[:, :, 1]], axis=2)
    against_imag = jnp.stack([partner[:, :, 1], partner[:, :, 0]], axis=2)
    bisp_real = jnp.einsum(
        "rvcbx,jvcbx->brj", product, against_real, preferred_element_type=jnp.float32
    )
    bisp_imag = jnp.einsum(
        "rvcbx,jvcbx->brj", product, against_imag, preferred_element_type=jnp.float32
    )
    return jnp.stack([bisp_real, bisp_imag], axis=-1)


def all_triads(row_coefs, col_coefs, weights, triad_pairs, block_size):
    row_split = row_coefs.reshape(row_coefs.shape[0], row_coefs.shape[1], 2, -1, row_coefs.shape[3])
    col_split = col_coefs.reshape(col_coefs.shape[0], col_coefs.shape[1], 2, -1, col_coefs.shape[3])
    pair_blocks = triad_pairs.reshape(-1, block_size, 2)
    result = lax.map(
        lambda pair_block: triad_block(row_split, col_split, weights, pair_block), pair_blocks
    )
    return result.reshape((triad_pairs.shape[0],) + result.shape[2:])


def slot_index(owner_counts, triad_total, most_owned):
    ending = jnp.cumsum(owner_counts)
    starting = ending - owner_counts
    positions = jnp.arange(triad_total, dtype=jnp.int32)
    owner_of = jnp.sum((positions[:, None] >= ending[None, :]).astype(jnp.int32), axis=1)
    owner_ids = jnp.arange(owner_counts.shape[0], dtype=jnp.int32)
    start_of = jnp.sum(
        jnp.where(owner_ids[None, :] == owner_of[:, None], starting[None, :], 0), axis=1
    )
    return owner_of * most_owned + positions - start_of


def local(snapshots, quad_weights, triad_pairs, owner_counts):
    basis = dft_table(snapshots.shape[2], FREQS)
    coeffs = jnp.einsum(
        "fs,ivsx->ivfx", basis, snapshots, preferred_element_type=jnp.float32
    ).astype(jnp.bfloat16)
    weights = quad_weights.astype(jnp.float32)
    weight_total = lax.psum(jnp.sum(weights * weights), "cell")
    triad_total = triad_pairs.shape[0]
    slot_ids = slot_index(owner_counts, triad_total, OWN_MOST)
    owner_total = owner_counts.shape[0]
    partners_all = lax.all_gather(coeffs, "real", axis=0, tiled=True)
    partial_value = all_triads(coeffs, partners_all, weights, triad_pairs, 2 * TRI_DEV)
    padded = (
        jnp.zeros((owner_total * OWN_MOST,) + partial_value.shape[1:], jnp.float32)
        .at[slot_ids]
        .set(partial_value)
    )
    padded = padded.reshape((owner_total, OWN_MOST) + partial_value.shape[1:])
    received = lax.all_to_all(padded, "cell", split_axis=0, concat_axis=0, tiled=True)
    summed = jnp.sum(received, axis=0)
    return summed / jnp.sqrt(weight_total)


def solution(mesh):
    return jax.shard_map(
        local,
        mesh=mesh,
        in_specs=(P("real", None, None, "cell"), P("cell"), P(), P()),
        out_specs=P("cell", "real", None, None),
        check_vma=False,
    )
```

profile of v0, /device:TPU:1, one launch (start us, length us, event | category | flops | bytes accessed | tf_op | source)
XLA Modules:
  0.0 530.6 jit_solution(3624221239324277138)
XLA Ops:
  8.3 4.3 convolution_convert_fusion
  13.2 85.9 %all-gather.2.cloned.1.call-done = bf16[8,2,128,2048]{3,2,1,0:T(8,128)(2,1)} async-done(((bf16[2,2,128,2048]{3,2,1,0:T(8,128)(2,1)}), bf16[8,2,128,2048]{3,2,1,0:T(8,128)(2,1)}) %all-gather.2.cloned.1.call-update) | async-done | bytes 8388624 | tf_op jit(solution)/shard_map/all_gather | solution.py:91
  99.1 332.3 %while.10 = (s32[]{:T(128)}, f32[16,32,2,8,2]{1,3,4,2,0:T(8,128)S(1)}, s32[16,32,2]{1,0,2:T(8,128)S(1)}, bf16[2,2,2,64,2048]{4,3,2,1,0:T(8,128)(2,1)}, f32[2048]...) while((s32[]{:T(128)}, f32[16,32,2,8,2]{1,3,4,2,0:T(8,128)S(1)}, s32[16,32,2]{1,0,2:T(8,128)S(1)}, ...), condition=%wide.region_5.6_spmd, body=%wide.region_4.5_spmd.sunk | while | flops 430185504 | bytes 105961104 | solution.py:63
  108.7 4.5 fusion.60
  113.3 6.4 %fusion.59 = f32[32,2,8,1]{2,1,0,3:T(2,128)S(1)} fusion(bf16[8,2,2,32,2048]{4,3,2,1,0:T(8,128)(2,1)} %get-tuple-element.137, bf16[2,2,2,32,2048]{4,3,2,1,0:T(8,128)(2,1)S(1)} %pad_maximum_fusion.6), kind=kOutput, calls=%fused_computation.11.clone.1 | convolution fusion | flops 8388608 | bytes 5244928 | tf_op jit(solution)/shard_map/while/body/eval_jaxpr/rvcbx,jvcbx->brj/dot_general | solution.py:53
  123.2 2.3 copy-done.1
  129.5 4.5 fusion.60
  134.1 6.4 %fusion.59 = f32[32,2,8,1]{2,1,0,3:T(2,128)S(1)} fusion(bf16[8,2,2,32,2048]{4,3,2,1,0:T(8,128)(2,1)} %get-tuple-element.137, bf16[2,2,2,32,2048]{4,3,2,1,0:T(8,128)(2,1)S(1)} %pad_maximum_fusion.6), kind=kOutput, calls=%fused_computation.11.clone.1 | convolution fusion | flops 8388608 | bytes 5244928 | tf_op jit(solution)/shard_map/while/body/eval_jaxpr/rvcbx,jvcbx->brj/dot_general | solution.py:53
  144.0 2.3 copy-done.1
  150.3 4.5 fusion.60
  154.9 6.4 %fusion.59 = f32[32,2,8,1]{2,1,0,3:T(2,128)S(1)} fusion(bf16[8,2,2,32,2048]{4,3,2,1,0:T(8,128)(2,1)} %get-tuple-element.137, bf16[2,2,2,32,2048]{4,3,2,1,0:T(8,128)(2,1)S(1)} %pad_maximum_fusion.6), kind=kOutput, calls=%fused_computation.11.clone.1 | convolution fusion | flops 8388608 | bytes 5244928 | tf_op jit(solution)/shard_map/while/body/eval_jaxpr/rvcbx,jvcbx->brj/dot_general | solution.py:53
  164.7 2.3 copy-done.1
  171.1 4.5 fusion.60
  175.6 6.4 %fusion.59 = f32[32,2,8,1]{2,1,0,3:T(2,128)S(1)} fusion(bf16[8,2,2,32,2048]{4,3,2,1,0:T(8,128)(2,1)} %get-tuple-element.137, bf16[2,2,2,32,2048]{4,3,2,1,0:T(8,128)(2,1)S(1)} %pad_maximum_fusion.6), kind=kOutput, calls=%fused_computation.11.clone.1 | convolution fusion | flops 8388608 | bytes 5244928 | tf_op jit(solution)/shard_map/while/body/eval_jaxpr/rvcbx,jvcbx->brj/dot_general | solution.py:53
  185.5 2.3 copy-done.1
  191.8 4.5 fusion.60
  196.4 6.4 %fusion.59 = f32[32,2,8,1]{2,1,0,3:T(2,128)S(1)} fusion(bf16[8,2,2,32,2048]{4,3,2,1,0:T(8,128)(2,1)} %get-tuple-element.137, bf16[2,2,2,32,2048]{4,3,2,1,0:T(8,128)(2,1)S(1)} %pad_maximum_fusion.6), kind=kOutput, calls=%fused_computation.11.clone.1 | convolution fusion | flops 8388608 | bytes 5244928 | tf_op jit(solution)/shard_map/while/body/eval_jaxpr/rvcbx,jvcbx->brj/dot_general | solution.py:53
  212.6 4.5 fusion.60
  217.2 6.4 %fusion.59 = f32[32,2,8,1]{2,1,0,3:T(2,128)S(1)} fusion(bf16[8,2,2,32,2048]{4,3,2,1,0:T(8,128)(2,1)} %get-tuple-element.137, bf16[2,2,2,32,2048]{4,3,2,1,0:T(8,128)(2,1)S(1)} %pad_maximum_fusion.6), kind=kOutput, calls=%fused_computation.11.clone.1 | convolution fusion | flops 8388608 | bytes 5244928 | tf_op jit(solution)/shard_map/while/body/eval_jaxpr/rvcbx,jvcbx->brj/dot_general | solution.py:53
  227.0 2.3 copy-done.1
  233.4 4.5 fusion.60
  237.9 6.4 %fusion.59 = f32[32,2,8,1]{2,1,0,3:T(2,128)S(1)} fusion(bf16[8,2,2,32,2048]{4,3,2,1,0:T(8,128)(2,1)} %get-tuple-element.137, bf16[2,2,2,32,2048]{4,3,2,1,0:T(8,128)(2,1)S(1)} %pad_maximum_fusion.6), kind=kOutput, calls=%fused_computation.11.clone.1 | convolution fusion | flops 8388608 | bytes 5244928 | tf_op jit(solution)/shard_map/while/body/eval_jaxpr/rvcbx,jvcbx->brj/dot_general | solution.py:53
  254.1 4.5 fusion.60
  258.7 6.4 %fusion.59 = f32[32,2,8,1]{2,1,0,3:T(2,128)S(1)} fusion(bf16[8,2,2,32,2048]{4,3,2,1,0:T(8,128)(2,1)} %get-tuple-element.137, bf16[2,2,2,32,2048]{4,3,2,1,0:T(8,128)(2,1)S(1)} %pad_maximum_fusion.6), kind=kOutput, calls=%fused_computation.11.clone.1 | convolution fusion | flops 8388608 | bytes 5244928 | tf_op jit(solution)/shard_map/while/body/eval_jaxpr/rvcbx,jvcbx->brj/dot_general | solution.py:53
  268.6 2.3 copy-done.1
  274.9 4.5 fusion.60
  279.5 6.4 %fusion.59 = f32[32,2,8,1]{2,1,0,3:T(2,128)S(1)} fusion(bf16[8,2,2,32,2048]{4,3,2,1,0:T(8,128)(2,1)} %get-tuple-element.137, bf16[2,2,2,32,2048]{4,3,2,1,0:T(8,128)(2,1)S(1)} %pad_maximum_fusion.6), kind=kOutput, calls=%fused_computation.11.clone.1 | convolution fusion | flops 8388608 | bytes 5244928 | tf_op jit(solution)/shard_map/while/body/eval_jaxpr/rvcbx,jvcbx->brj/dot_general | solution.py:53
  289.3 2.3 copy-done.1
  295.7 4.5 fusion.60
  300.2 6.4 %fusion.59 = f32[32,2,8,1]{2,1,0,3:T(2,128)S(1)} fusion(bf16[8,2,2,32,2048]{4,3,2,1,0:T(8,128)(2,1)} %get-tuple-element.137, bf16[2,2,2,32,2048]{4,3,2,1,0:T(8,128)(2,1)S(1)} %pad_maximum_fusion.6), kind=kOutput, calls=%fused_computation.11.clone.1 | convolution fusion | flops 8388608 | bytes 5244928 | tf_op jit(solution)/shard_map/while/body/eval_jaxpr/rvcbx,jvcbx->brj/dot_general | solution.py:53
  316.4 4.5 fusion.60
  321.0 6.4 %fusion.59 = f32[32,2,8,1]{2,1,0,3:T(2,128)S(1)} fusion(bf16[8,2,2,32,2048]{4,3,2,1,0:T(8,128)(2,1)} %get-tuple-element.137, bf16[2,2,2,32,2048]{4,3,2,1,0:T(8,128)(2,1)S(1)} %pad_maximum_fusion.6), kind=kOutput, calls=%fused_computation.11.clone.1 | convolution fusion | flops 8388608 | bytes 5244928 | tf_op jit(solution)/shard_map/while/body/eval_jaxpr/rvcbx,jvcbx->brj/dot_general | solution.py:53
  330.9 2.3 copy-done.1
  337.2 4.5 fusion.60
  341.8 6.4 %fusion.59 = f32[32,2,8,1]{2,1,0,3:T(2,128)S(1)} fusion(bf16[8,2,2,32,2048]{4,3,2,1,0:T(8,128)(2,1)} %get-tuple-element.137, bf16[2,2,2,32,2048]{4,3,2,1,0:T(8,128)(2,1)S(1)} %pad_maximum_fusion.6), kind=kOutput, calls=%fused_computation.11.clone.1 | convolution fusion | flops 8388608 | bytes 5244928 | tf_op jit(solution)/shard_map/while/body/eval_jaxpr/rvcbx,jvcbx->brj/dot_general | solution.py:53
  358.0 4.5 fusion.60
  362.5 6.4 %fusion.59 = f32[32,2,8,1]{2,1,0,3:T(2,128)S(1)} fusion(bf16[8,2,2,32,2048]{4,3,2,1,0:T(8,128)(2,1)} %get-tuple-element.137, bf16[2,2,2,32,2048]{4,3,2,1,0:T(8,128)(2,1)S(1)} %pad_maximum_fusion.6), kind=kOutput, calls=%fused_computation.11.clone.1 | convolution fusion | flops 8388608 | bytes 5244928 | tf_op jit(solution)/shard_map/while/body/eval_jaxpr/rvcbx,jvcbx->brj/dot_general | solution.py:53
  372.4 2.3 copy-done.1
  378.7 4.5 fusion.60
  383.3 6.4 %fusion.59 = f32[32,2,8,1]{2,1,0,3:T(2,128)S(1)} fusion(bf16[8,2,2,32,2048]{4,3,2,1,0:T(8,128)(2,1)} %get-tuple-element.137, bf16[2,2,2,32,2048]{4,3,2,1,0:T(8,128)(2,1)S(1)} %pad_maximum_fusion.6), kind=kOutput, calls=%fused_computation.11.clone.1 | convolution fusion | flops 8388608 | bytes 5244928 | tf_op jit(solution)/shard_map/while/body/eval_jaxpr/rvcbx,jvcbx->brj/dot_general | solution.py:53
  393.2 2.3 copy-done.1
  399.5 4.5 fusion.60
  404.1 6.4 %fusion.59 = f32[32,2,8,1]{2,1,0,3:T(2,128)S(1)} fusion(bf16[8,2,2,32,2048]{4,3,2,1,0:T(8,128)(2,1)} %get-tuple-element.137, bf16[2,2,2,32,2048]{4,3,2,1,0:T(8,128)(2,1)S(1)} %pad_maximum_fusion.6), kind=kOutput, calls=%fused_computation.11.clone.1 | convolution fusion | flops 8388608 | bytes 5244928 | tf_op jit(solution)/shard_map/while/body/eval_jaxpr/rvcbx,jvcbx->brj/dot_general | solution.py:53
  420.3 4.5 fusion.60
  424.8 6.4 %fusion.59 = f32[32,2,8,1]{2,1,0,3:T(2,128)S(1)} fusion(bf16[8,2,2,32,2048]{4,3,2,1,0:T(8,128)(2,1)} %get-tuple-element.137, bf16[2,2,2,32,2048]{4,3,2,1,0:T(8,128)(2,1)S(1)} %pad_maximum_fusion.6), kind=kOutput, calls=%fused_computation.11.clone.1 | convolution fusion | flops 8388608 | bytes 5244928 | tf_op jit(solution)/shard_map/while/body/eval_jaxpr/rvcbx,jvcbx->brj/dot_general | solution.py:53
  432.7 13.7 %scatter_fusion = f32[1024,2,8,2]{2,3,1,0:T(2,128)S(1)} fusion(f32[1024,2,8,2]{2,3,1,0:T(2,128)S(1)} %broadcast_in_dim.19, s32[512]{0:T(512)S(1)} %bitcast.107, f32[512,2,8,2]{2,3,1,0:T(2,128)S(1)} %bitcast.102), kind=kCustom, calls=%fused_computation | custom fusion | bytes 198656 | tf_op jit(solution)/shard_map/scatter | solution.py:96
  449.3 7.7 %all-to-all-start = ((f32[32,1,1024]{2,1,0:T(1,128)}), f32[32,1,1024]{2,1,0:T(1,128)S(1)}, u32[]{:S(2)}, u32[]{:S(2)}) async-start(f32[32,1,1024]{2,1,0:T(1,128)} %reshape.107), calls=%async_computation | async-start | bytes 262144 | tf_op jit(solution)/shard_map/all_to_all | solution.py:99
  457.6 63.1 %psum.7 = f32[]{:T(128)} all-reduce(f32[]{:T(128)} %multiply_reduce_fusion), channel_id=1, replica_groups=mesh['real'=4,'cell'=32] {'cell'}, use_global_device_ids=true, to_apply=%region_9.10 | all-reduce | flops 1 | bytes 8 | tf_op jit(solution)/shard_map/psum | solution.py:87
  (281 shorter events, 141.5 us)
Async XLA Ops:
  6.5 92.6 %all-gather.2.cloned.1.call-start = ((), (), s32[]{:S(2)}) async-start(), calls=%async_computation.1 | async-start | bytes 10485760 | tf_op jit(solution)/shard_map/all_gather | solution.py:91
  8.3 4.4 copy-start.3
  8.3 4.4 copy-start.2
  8.3 4.4 copy-start.4
  99.1 2.2 copy-start
  101.4 3.4 copy-start.1
  119.9 2.3 copy-start
  122.1 3.4 copy-start.1
  140.6 2.3 copy-start
  142.9 3.4 copy-start.1
  161.4 2.3 copy-start
  163.7 3.4 copy-start.1
  182.2 2.3 copy-start
  184.4 3.4 copy-start.1
  202.9 2.3 copy-start
  205.2 3.4 copy-start.1
  223.7 2.3 copy-start
  226.0 3.4 copy-start.1
  244.5 2.3 copy-start
  246.7 3.4 copy-start.1
  265.2 2.3 copy-start
  267.5 3.4 copy-start.1
  286.0 2.3 copy-start
  288.3 3.4 copy-start.1
  306.8 2.3 copy-start
  309.0 3.4 copy-start.1
  327.5 2.3 copy-start
  329.8 3.4 copy-start.1
  348.3 2.3 copy-start
  350.6 3.4 copy-start.1
  369.1 2.3 copy-start
  371.3 3.4 copy-start.1
  389.8 2.3 copy-start
  392.1 3.4 copy-start.1
  410.6 2.3 copy-start
  412.9 3.4 copy-start.1
  449.3 72.1 %all-to-all-start = ((f32[32,1,1024]{2,1,0:T(1,128)}), f32[32,1,1024]{2,1,0:T(1,128)S(1)}, u32[]{:S(2)}, u32[]{:S(2)}) async-start(f32[32,1,1024]{2,1,0:T(1,128)} %reshape.107), calls=%async_computation | async-start | bytes 262144 | tf_op jit(solution)/shard_map/all_to_all | solution.py:99
Sparse Core Ops, SparseCore 0:
  12.7 86.3 all-gather.1
where the time goes:
time: 536 us; the launch traced here: 531 us
  matrix products  244 us (46%)
  waiting for transfers between devices  85.9 us (16%)
  blocking collectives  63.1 us (12%)
  local copies, waits for them, and re-layouts  58.9 us (11%)
  other arithmetic  55.4 us (10%)
  between operations  14.9 us (3%)
  starting transfers between devices  7.7 us (1%)
    dot_general x16, matrix products, triad_block(): jnp.einsum('rvcbx,jvcbx->brj', product, against_imag, preferred_element_t...  103 us
    all_gather x1, waiting for transfers between devices, local(): partners_all = lax.all_gather(coeffs, 'real', axis=0, tiled=True)  85.9 us
    dot_general x16, matrix products, triad_block(): jnp.einsum('rvcbx,jvcbx->brj', product, against_real, preferred_element_t...  72.1 us
    dot_general x48, matrix products, select_bins(): jnp.einsum('bf,ivcfx->ivcbx', onehot, coefs, preferred_element_type=jnp.f...  64.1 us
    psum x1, blocking collectives, local(): weight_total = lax.psum(jnp.sum(weights * weights), 'cell')  63.1 us
    while x64, local copies, waits for them, and re-layouts  37 us
    another operation x16, other arithmetic, triad_block(): against_real = jnp.stack([partner[:, :, 0], -partner[:, :, 1]], axis=2)  36.7 us
    scatter x1, local copies, waits for them, and re-layouts, local(): padded = jnp.zeros((owner_total * OWN_MOST,) + partial_value.shape[1:], j...  13.7 us
  transfers between devices with their start and end apart: 2, of which 1 were waited for; matrix products, arithmetic and copies ran while one was open for 0% of the time, Pallas kernels for 0%

commit v1 on v0

v1 whole, which is shorter than its diff:
```python
import functools

import jax
import jax.numpy as jnp
import numpy as np
from jax import lax
from jax.experimental import pallas as pl
from jax.experimental.pallas import tpu as pltpu
from jax.sharding import PartitionSpec as P

SNAPS = 256
FREQS = 64
REALS = 8
TRIADS = 512
OWN_MOST = 32
N_REAL = 4
N_CELL = 32
XQ = 512
TB = 32
WIN = 16
ROWS = 9
VMEM = 56 * 1024 * 1024


def dft_table():
    times = np.arange(SNAPS)
    bins = np.arange(FREQS)
    window = 0.5 - 0.5 * np.cos(2.0 * np.pi * times / SNAPS)
    norm = np.sqrt(np.sum(window * window))
    phases = 2.0 * np.pi * ((bins[:, None] * times[None, :]) % SNAPS) / SNAPS
    table = np.concatenate([window * np.cos(phases), -window * np.sin(phases)], axis=0) / norm
    return jnp.asarray(table.astype(np.float32)).astype(jnp.bfloat16)


def dft_kernel(n, where_ref, basis_ref, *refs):
    for s in range(n):
        refs[n + s][0, 0] = jnp.dot(
            basis_ref[...], refs[s][0, 0], preferred_element_type=jnp.float32
        ).astype(jnp.bfloat16)


def dft(where, basis, snapshots, shifts):
    n = len(shifts)

    def source(s):
        return lambda r, v, where: (r, v, 0, lax.rem(where[0] + s, N_REAL))

    return pl.pallas_call(
        functools.partial(dft_kernel, n),
        grid_spec=pltpu.PrefetchScalarGridSpec(
            num_scalar_prefetch=1,
            grid=(2, 2),
            in_specs=[pl.BlockSpec((2 * FREQS, SNAPS), lambda r, v, where: (0, 0))]
            + [pl.BlockSpec((1, 1, SNAPS, XQ), source(s)) for s in shifts],
            out_specs=[pl.BlockSpec((1, 1, 2 * FREQS, XQ), lambda r, v, where: (r, v, 0, 0)) for s in shifts],
        ),
        out_shape=[jax.ShapeDtypeStruct((2, 2, 2 * FREQS, XQ), jnp.bfloat16) for s in shifts],
        compiler_params=pltpu.CompilerParams(vmem_limit_bytes=VMEM),
        cost_estimate=pl.CostEstimate(
            flops=2 * 4 * n * 2 * FREQS * SNAPS * XQ, bytes_accessed=4 * n * 3 * FREQS * 2 * XQ * 2, transcendentals=0
        ),
    )(where, basis, *([snapshots] * n))


def triad_kernel(where_ref, packed_ref, p0, p1, p2, p3, w_ref, out_ref, cf, wc, part, left_a, left_b, full, acc):
    vx = 2 * XQ
    me = where_ref[0]
    for s, piece in enumerate((p0, p1, p2, p3)):
        group = lax.rem(me + N_REAL - s, N_REAL)
        for r in range(2):
            for v in range(2):
                for q in range(XQ // 128):
                    cf[v * (XQ // 128) + q, pl.ds(2 * group + r, 2 * FREQS, stride=REALS), :] = piece[
                        r, v, :, q * 128 : (q + 1) * 128
                    ].astype(jnp.float32)
    tiles = vx // 128
    weights = w_ref[...].astype(jnp.float32)

    def prepare(m, carry):
        re = pl.ds(pl.multiple_of(m * REALS, REALS), REALS)
        im = pl.ds(pl.multiple_of((m + FREQS) * REALS, REALS), REALS)
        rows = pl.ds(pl.multiple_of(m * 2 * REALS, 2 * REALS), 2 * REALS)
        for q in range(tiles):
            at = q % (XQ // 128) * 128
            weight = weights[:, at : at + 128]
            a, b = cf[q, re, :], cf[q, im, :]
            wc[q, re, :] = a * weight
            wc[q, im, :] = b * weight
            part[rows, q * 128 : (q + 1) * 128] = jnp.concatenate([a, b], axis=0).astype(jnp.bfloat16)
            part[rows, vx + q * 128 : vx + (q + 1) * 128] = jnp.concatenate([b, -a], axis=0).astype(jnp.bfloat16)
        return carry

    lax.fori_loop(0, FREQS, prepare, 0, unroll=4)
    acc[...] = jnp.zeros_like(acc)
    lane_group = lax.broadcasted_iota(jnp.int32, (REALS, 128), 1) // (2 * REALS)

    def bins_of(t):
        word = packed_ref[t]
        return word & 63, (word >> 6) & 63, word >> 12

    def build(left, block):
        for pair in range(TB // 2):
            rows = slice(2 * REALS * pair, 2 * REALS * (pair + 1))
            slices = []
            for h in range(2):
                k, l, _ = bins_of(block * TB + 2 * pair + h)
                slices.append([pl.ds(pl.multiple_of(n * REALS, REALS), REALS) for n in (k, k + FREQS, l, l + FREQS)])
            for q in range(tiles):
                reals, imags = [], []
                for kr, ki, lr, li in slices:
                    ak, bk, al, bl = wc[q, kr, :], wc[q, ki, :], cf[q, lr, :], cf[q, li, :]
                    reals.append(ak * al - bk * bl)
                    imags.append(ak * bl + bk * al)
                left[rows, q * 128 : (q + 1) * 128] = jnp.concatenate(reals, axis=0).astype(jnp.bfloat16)
                left[rows, vx + q * 128 : vx + (q + 1) * 128] = jnp.concatenate(imags, axis=0).astype(jnp.bfloat16)

    def window(left, block, first):
        rows = pl.ds(pl.multiple_of(first * 2 * REALS, 2 * REALS), WIN * 2 * REALS)
        prod = lax.dot_general(
            left[...], part[rows, :], (((1,), (1,)), ((), ())), preferred_element_type=jnp.float32
        )
        full[0] = prod[:, :128]
        full[1] = prod[:, 128:]
        for i in range(TB):
            k, l, slot = bins_of(block * TB + i)
            at = k + l - first
            inside = jnp.logical_and(at >= 0, at < WIN)
            at = lax.rem(jnp.maximum(at, 0), WIN)
            tile = full[at // 8, pl.ds(i * REALS, REALS), :]
            turn = lax.rem(lax.rem(slot, 8) - lax.rem(at, 8) + 8, 8) * (2 * REALS)
            tile = pltpu.roll(tile, turn, 1)
            want = jnp.where(inside, lax.rem(slot, 8), -1)
            pltpu.store(
                acc.at[pl.ds(pl.multiple_of((slot // 8) * REALS, REALS), REALS), :], tile, mask=lane_group == want
            )

    def use(left, block):
        k, l, _ = bins_of(block * TB)
        low = k + l
        k, l, _ = bins_of(block * TB + TB - 1)
        high = k + l
        window(left, block, jnp.minimum(low, FREQS - WIN))

        def more(first):
            window(left, block, jnp.minimum(first, FREQS - WIN))
            return first + WIN

        lax.while_loop(lambda first: first <= high, more, low + WIN)

    blocks = TRIADS // TB
    build(left_a, 0)

    def step(i, carry):
        build(left_b, 2 * i + 1)
        use(left_a, 2 * i)
        build(left_a, jnp.minimum(2 * i + 2, blocks - 1))
        use(left_b, 2 * i + 1)
        return carry

    lax.fori_loop(0, blocks // 2, step, 0)

    own = w_ref[...].astype(jnp.float32)
    square = jnp.sum(own * own, axis=1, keepdims=True)
    square = jnp.broadcast_to(square, (1, 128))
    for o in range(N_CELL):
        for y in range(N_REAL):
            to = ROWS * (o * N_REAL + y)
            for r in range(2):
                out_ref[to + 4 * r : to + 4 * r + 4, :] = acc[pl.ds(o * 32 + 2 * y + r, 4, stride=REALS), :]
            out_ref[to + 8 : to + 9, :] = square


def triads(where, packed, pieces, quad_weights):
    vx = 2 * XQ
    whole = pl.BlockSpec((2, 2, 2 * FREQS, XQ), lambda i, where, packed: (0, 0, 0, 0))
    return pl.pallas_call(
        triad_kernel,
        grid_spec=pltpu.PrefetchScalarGridSpec(
            num_scalar_prefetch=2,
            grid=(1,),
            in_specs=[whole] * 4 + [pl.BlockSpec((1, XQ), lambda i, where, packed: (0, where[0]))],
            out_specs=pl.BlockSpec((N_CELL * N_REAL * ROWS, 128), lambda i, where, packed: (0, 0)),
            scratch_shapes=[
                pltpu.VMEM((vx // 128, 2 * FREQS * REALS, 128), jnp.float32),
                pltpu.VMEM((vx // 128, 2 * FREQS * REALS, 128), jnp.float32),
                pltpu.VMEM((2 * FREQS * REALS, 2 * vx), jnp.bfloat16),
                pltpu.VMEM((TB * REALS, 2 * vx), jnp.bfloat16),
                pltpu.VMEM((TB * REALS, 2 * vx), jnp.bfloat16),
                pltpu.VMEM((2, TB * REALS, 128), jnp.float32),
                pltpu.VMEM((N_CELL * OWN_MOST, 128), jnp.float32),
            ],
        ),
        out_shape=jax.ShapeDtypeStruct((N_CELL * N_REAL * ROWS, 128), jnp.float32),
        compiler_params=pltpu.CompilerParams(vmem_limit_bytes=VMEM),
        cost_estimate=pl.CostEstimate(flops=10_000_000_000, bytes_accessed=4 * 1024 * 1024, transcendentals=0),
    )(where, packed, *pieces, quad_weights)


def sorted_words(triad_pairs, owner_counts):
    ids = jnp.arange(TRIADS, dtype=jnp.int32)
    owners = jnp.arange(N_CELL, dtype=jnp.int32)
    ending = jnp.sum(jnp.where(owners[None, :] <= owners[:, None], owner_counts[None, :], 0), axis=1)
    past = ids[:, None] >= ending[None, :]
    owner = jnp.sum(past.astype(jnp.int32), axis=1)
    start = jnp.sum(jnp.where(past, owner_counts[None, :], 0), axis=1)
    slot = owner * OWN_MOST + ids - start
    first, second = triad_pairs[:, 0], triad_pairs[:, 1]
    key = (first + second) * TRIADS + ids
    rank = jnp.sum((key[None, :] < key[:, None]).astype(jnp.int32), axis=1)
    word = first + second * FREQS + slot * FREQS * FREQS
    return jnp.sum(jnp.where(rank[None, :] == ids[:, None], word[None, :], 0), axis=1)


def local(snapshots, quad_weights, triad_pairs, owner_counts):
    basis = dft_table()
    where = lax.axis_index("real").astype(jnp.int32).reshape(1)
    away = dft(where, basis, snapshots, (2, 1, 3))
    arrived = [
        lax.ppermute(piece, "real", [(i, (i + s) % N_REAL) for i in range(N_REAL)])
        for piece, s in zip(away, (2, 1, 3))
    ]
    (own,) = dft(where, basis, snapshots, (0,))
    words = sorted_words(triad_pairs, owner_counts)
    sums = triads(where, words, (own, arrived[1], arrived[0], arrived[2]), quad_weights.reshape(1, -1))
    sums = sums.reshape(N_CELL * N_REAL, 1, ROWS * 128)
    received = lax.all_to_all(sums, ("cell", "real"), split_axis=0, concat_axis=0, tiled=True)
    total = jnp.sum(received, axis=(0, 1))
    values = total[: 8 * 128].reshape(2, 4, 8, 2, REALS)
    values = jnp.transpose(values, (1, 2, 0, 4, 3)).reshape(OWN_MOST, 2, REALS, 2)
    return values / jnp.sqrt(total[8 * 128])


def solution(mesh):
    return jax.shard_map(
        local,
        mesh=mesh,
        in_specs=(P("real", None, None, "cell"), P("cell"), P(), P()),
        out_specs=P("cell", "real", None, None),
        check_vma=False,
    )
```

time: 536 us -> 91.1 us (0.17)
  matrix products: 244 us -> 0 us
  waiting for transfers between devices: 85.9 us -> 16.8 us
  local copies, waits for them, and re-layouts: 58.9 us -> 2.31 us
  other arithmetic: 55.4 us -> 1.63 us
  Pallas kernels: 0 us -> 38.1 us
  blocking collectives: 63.1 us -> 25.3 us
  between operations: 14.9 us -> 0.74 us
    dot_general x81 -> x0, matrix products: 244 us -> none  [the longest x16 103 us: triad_block(): jnp.einsum('rvcbx,jvcbx->brj', product, against_imag, preferred_element_t...]
    all_gather x1 -> x0, waiting for transfers between devices: 85.9 us -> none  [local(): partners_all = lax.all_gather(coeffs, 'real', axis=0, tiled=True)]
    psum x1 -> x0, blocking collectives: 63.1 us -> none  [local(): weight_total = lax.psum(jnp.sum(weights * weights), 'cell')]
    another operation x51 -> x0, other arithmetic: 46.1 us -> none  [the longest x16 36.7 us: triad_block(): against_real = jnp.stack([partner[:, :, 0], -partner[:, :, 1]], axis=2)]
    pallas_call x0 -> x3, Pallas kernels: none -> 38.1 us  [the longest x1 30.3 us: triads(): pl.pallas_call(triad_kernel, grid_spec=pltpu.PrefetchScalarGridSpec(num_s...]
    while x64 -> x0, local copies, waits for them, and re-layouts: 37 us -> none
    all_to_all x0 -> x1, blocking collectives: none -> 25.3 us  [local(): lax.all_to_all(sums, ('cell', 'real'), split_axis=0, concat_axis=0, tiled...]
    ppermute x0 -> x3, waiting for transfers between devices: none -> 16.8 us  [local(): lax.ppermute(piece, 'real', [(i, (i + s) % N_REAL) for i in range(N_REAL)])]
  transfers between devices with their start and end apart: 2 -> 3, of which waited for: 1 -> 2; matrix products, arithmetic and copies ran while one was open for 0% -> 1% of each run, Pallas kernels for 0% -> 4%
where the time goes in v1:
time: 91.1 us; the launch traced here: 90.8 us
  Pallas kernels  38.1 us (42%)
  blocking collectives  25.3 us (28%)
  waiting for transfers between devices  16.8 us (18%)
  starting transfers between devices  5.81 us (6%)
  local copies, waits for them, and re-layouts  2.31 us (3%)
  other arithmetic  1.63 us (2%)
    pallas_call x1, Pallas kernels, triads(): pl.pallas_call(triad_kernel, grid_spec=pltpu.PrefetchScalarGridSpec(num_s...  30.3 us
    all_to_all x1, blocking collectives, local(): lax.all_to_all(sums, ('cell', 'real'), split_axis=0, concat_axis=0, tiled...  25.3 us
    ppermute x3, waiting for transfers between devices, local(): lax.ppermute(piece, 'real', [(i, (i + s) % N_REAL) for i in range(N_REAL)])  16.8 us
    pallas_call x2, Pallas kernels, dft(): pl.pallas_call(functools.partial(dft_kernel, n), grid_spec=pltpu.Prefetch...  7.85 us
    ppermute x3, starting transfers between devices, local(): lax.ppermute(piece, 'real', [(i, (i + s) % N_REAL) for i in range(N_REAL)])  5.81 us
  transfers between devices with their start and end apart: 3, of which 2 were waited for; matrix products, arithmetic and copies ran while one was open for 1% of the time, Pallas kernels for 4%

profile of v1, /device:TPU:1, one launch (start us, length us, event | category | flops | bytes accessed | tf_op | source)
XLA Modules:
  0.0 90.8 jit_solution(11795749776372694139)
XLA Ops:
  0.0 0.0 copy-start.1
  0.0 0.0 copy-start
  0.0 4.2 %shard_map.56 = (bf16[2,2,128,512]{3,2,1,0:T(8,128)(2,1)}, bf16[2,2,128,512]{3,2,1,0:T(8,128)(2,1)}, bf16[2,2,128,512]{3,2,1,0:T(8,128)(2,1)}) custom-call(s32[1]{0:T(128)} %bitcast.where_ref, bf16[128,256]{1,0:T(8,128)(2,1)} %constant.22.basis_ref, bf16[2,2,256,2048]{3,2,1,0:T(8,128)(2,1)} %refs_2_.1, bf16[2,2,256,2048]{3,2,1,0:T(8,128)(2,1)} %refs_2_.1, ...), custom_call_target="tpu_custom_call" | custom-call | flops 402653184 | bytes 4718592 | tf_op jit(solution)/shard_map/pallas_call | solution.py:48
  4.2 2.1 %collective-permute-start = (bf16[2,2,128,512]{3,2,1,0:T(8,128)(2,1)}, bf16[2,2,128,512]{3,2,1,0:T(8,128)(2,1)S(1)}, u32[]{:S(2)}, u32[]{:S(2)}) collective-permute-start(bf16[2,2,128,512]{3,2,1,0:T(8,128)(2,1)} %get-tuple-element.8), channel_id=1, source_target_pairs={{0,32},{32,64},{64,96},{96,0},{1,33},{33,65},{65,97},{97,1},{2,34}... | collective-permute-start | bytes 1572872 | tf_op jit(solution)/shard_map/ppermute | solution.py:219
  6.4 2.6 %collective-permute-start.1 = (bf16[2,2,128,512]{3,2,1,0:T(8,128)(2,1)}, bf16[2,2,128,512]{3,2,1,0:T(8,128)(2,1)S(1)}, u32[]{:S(2)}, u32[]{:S(2)}) collective-permute-start(bf16[2,2,128,512]{3,2,1,0:T(8,128)(2,1)} %get-tuple-element.9), channel_id=1, source_target_pairs={{0,64},{32,96},{64,0},{96,32},{1,65},{33,97},{65,1},{97,33},{2,66}... | collective-permute-start | bytes 1572872 | tf_op jit(solution)/shard_map/ppermute | solution.py:219
  9.0 1.1 %collective-permute-start.2 = (bf16[2,2,128,512]{3,2,1,0:T(8,128)(2,1)}, bf16[2,2,128,512]{3,2,1,0:T(8,128)(2,1)S(1)}, u32[]{:S(2)}, u32[]{:S(2)}) collective-permute-start(bf16[2,2,128,512]{3,2,1,0:T(8,128)(2,1)} %get-tuple-element.10), channel_id=1, source_target_pairs={{0,96},{32,0},{64,32},{96,64},{1,97},{33,1},{65,33},{97,65},{2,98}... | collective-permute-start | bytes 1572872 | tf_op jit(solution)/shard_map/ppermute | solution.py:219
  10.1 0.0 copy-done.1
  10.1 0.1 select_reduce_fusion.2
  10.2 0.0 copy-done
  10.2 0.1 convert_reduce_fusion.1
  10.3 3.6 %shard_map.55.p0 = bf16[2,2,128,512]{3,2,1,0:T(8,128)(2,1)} custom-call(s32[1]{0:T(128)} %bitcast.where_ref, bf16[128,256]{1,0:T(8,128)(2,1)} %constant.22.basis_ref, bf16[2,2,256,2048]{3,2,1,0:T(8,128)(2,1)} %refs_2_.1), custom_call_target="tpu_custom_call" | custom-call | flops 134217728 | bytes 1572864 | tf_op jit(solution)/shard_map/pallas_call | solution.py:48
  13.9 0.2 convert_reduce_fusion
  14.2 0.8 select_reduce_fusion.packed_ref
  14.9 4.6 %collective-permute-done.p1 = bf16[2,2,128,512]{3,2,1,0:T(8,128)(2,1)S(1)} collective-permute-done((bf16[2,2,128,512]{3,2,1,0:T(8,128)(2,1)}, bf16[2,2,128,512]{3,2,1,0:T(8,128)(2,1)S(1)}, u32[]{:S(2)}, u32[]{:S(2)}) %collective-permute-start) | collective-permute-done | bytes 524320 | tf_op jit(solution)/shard_map/ppermute | solution.py:219
  19.5 0.0 copy-start.2
  19.5 12.3 %collective-permute-done.1.p2 = bf16[2,2,128,512]{3,2,1,0:T(8,128)(2,1)S(1)} collective-permute-done((bf16[2,2,128,512]{3,2,1,0:T(8,128)(2,1)}, bf16[2,2,128,512]{3,2,1,0:T(8,128)(2,1)S(1)}, u32[]{:S(2)}, u32[]{:S(2)}) %collective-permute-start.1) | collective-permute-done | bytes 524320 | tf_op jit(solution)/shard_map/ppermute | solution.py:219
  31.8 0.0 copy-start.3
  31.8 0.0 collective-permute-done.2.p3
  31.8 0.0 copy-start.4
  31.8 0.0 copy-done.2
  31.8 0.8 copy-done.3
  32.5 0.2 copy-done.4
  32.7 30.3 %shard_map.57 = f32[1152,128]{1,0:T(8,128)} custom-call(s32[1]{0:T(128)} %bitcast.where_ref, s32[512]{0:T(512)} %select_reduce_fusion.packed_ref, bf16[2,2,128,512]{3,2,1,0:T(8,128)(2,1)} %shard_map.55.p0, bf16[2,2,128,512]{3,2,1,0:T(8,128)(2,1)} %copy-done.2, bf16[2,2,128,512]{3,2,1,0:T(8,128)(2,1)} %copy-done.3, bf16[2,2,128,512]{3,2,1,0:T(8,128)(2,1)} %copy-done.4, ...), custom_call_target="tpu_custom_call" | custom-call | flops 10000000000 | bytes 4194304 | tf_op jit(solution)/shard_map/pallas_call | solution.py:176
  63.0 25.3 %all_to_all.5 = f32[128,1,1152]{2,1,0:T(1,128)S(1)} all-to-all(f32[128,1,1152]{2,1,0:T(1,128)} %bitcast.10), channel_id=1, replica_groups=mesh['real'=4,'cell'=32] {'cell','real'}, dimensions={0} | all-to-all | bytes 1179648 | tf_op jit(solution)/shard_map/all_to_all | solution.py:226
  88.3 0.4 reduce_sum.59
  88.7 0.5 slice.17
  89.9 0.1 div.17
  90.1 0.7 copy.10
  (3 shorter events, 0.0 us)
Async XLA Ops:
  0.0 10.1 %copy-start.1 = (s32[32]{0:T(128)S(1)}, s32[32]{0:T(128)}, u32[]{:S(2)}) copy-start(s32[32]{0:T(128)} %param.8) | copy-start | bytes 388
  0.0 10.2 %copy-start = (s32[512,2]{0,1:T(2,128)S(1)}, s32[512,2]{0,1:T(2,128)}, u32[]{:S(2)}) copy-start(s32[512,2]{0,1:T(2,128)} %param.7) | copy-start | bytes 12292
  4.2 15.3 %collective-permute-start = (bf16[2,2,128,512]{3,2,1,0:T(8,128)(2,1)}, bf16[2,2,128,512]{3,2,1,0:T(8,128)(2,1)S(1)}, u32[]{:S(2)}, u32[]{:S(2)}) collective-permute-start(bf16[2,2,128,512]{3,2,1,0:T(8,128)(2,1)} %get-tuple-element.8), channel_id=1, source_target_pairs={{0,32},{32,64},{64,96},{96,0},{1,33},{33,65},{65,97},{97,1},{2,34}... | collective-permute-start | bytes 1572872 | tf_op jit(solution)/shard_map/ppermute | solution.py:219
  6.4 25.4 %collective-permute-start.1 = (bf16[2,2,128,512]{3,2,1,0:T(8,128)(2,1)}, bf16[2,2,128,512]{3,2,1,0:T(8,128)(2,1)S(1)}, u32[]{:S(2)}, u32[]{:S(2)}) collective-permute-start(bf16[2,2,128,512]{3,2,1,0:T(8,128)(2,1)} %get-tuple-element.9), channel_id=1, source_target_pairs={{0,64},{32,96},{64,0},{96,32},{1,65},{33,97},{65,1},{97,33},{2,66}... | collective-permute-start | bytes 1572872 | tf_op jit(solution)/shard_map/ppermute | solution.py:219
  9.0 22.8 %collective-permute-start.2 = (bf16[2,2,128,512]{3,2,1,0:T(8,128)(2,1)}, bf16[2,2,128,512]{3,2,1,0:T(8,128)(2,1)S(1)}, u32[]{:S(2)}, u32[]{:S(2)}) collective-permute-start(bf16[2,2,128,512]{3,2,1,0:T(8,128)(2,1)} %get-tuple-element.10), channel_id=1, source_target_pairs={{0,96},{32,0},{64,32},{96,64},{1,97},{33,1},{65,33},{97,65},{2,98}... | collective-permute-start | bytes 1572872 | tf_op jit(solution)/shard_map/ppermute | solution.py:219
  19.5 12.3 %copy-start.2 = (bf16[2,2,128,512]{3,2,1,0:T(8,128)(2,1)}, bf16[2,2,128,512]{3,2,1,0:T(8,128)(2,1)S(1)}, u32[]{:S(2)}) copy-start(bf16[2,2,128,512]{3,2,1,0:T(8,128)(2,1)S(1)} %collective-permute-done.p1) | copy-start | bytes 1572868
  31.8 0.8 copy-start.3
  31.8 1.0 %copy-start.4 = (bf16[2,2,128,512]{3,2,1,0:T(8,128)(2,1)}, bf16[2,2,128,512]{3,2,1,0:T(8,128)(2,1)S(1)}, u32[]{:S(2)}) copy-start(bf16[2,2,128,512]{3,2,1,0:T(8,128)(2,1)S(1)} %collective-permute-done.2.p3) | copy-start | bytes 1572868
